TPU v7x, 32 devices: a whole 2x2x4 slice. The times are simulated.
32 devices in a mesh: space: 8 (over y, x, core), ens: 4 (over z).
Axes of the slice: x: 2, y: 2, z: 4, core: 2. Of those that a mesh axis runs over, the one named last changes fastest.
Arguments:
- fields: bfloat16 [8, 45, 64, 360], P('ens', None, 'space'), may hold values from -6 to 6
- observed: bfloat16 [45, 64, 360], P(None, 'space'), may hold values from -8 to 8
- kernel_one: bfloat16 [9, 45, 5, 45], replicated, may hold values from -0.375 to 0.375
- bias_one: float32 [45], replicated, may hold values from -3 to 3
- kernel_two: bfloat16 [9, 45, 5, 45], replicated, may hold values from -0.375 to 0.375
- bias_two: float32 [45], replicated, may hold values from -3 to 3
- band_offset: int32 [64], replicated, may hold values from -4 to 3, as said below
- band_width: int32 [64], replicated, may hold values from 2 to 9
Outputs:
- score_grad: bfloat16 [8, 45, 64, 360], P('ens', None, 'space')
Inputs may be any that keep to these rules, and one draw needn't show every extreme that they name: band_offset[i] + band_width[i] - 1 <= 4 for every latitude.
All inputs are finite; a program needn't handle non-finite values.
Results may differ from a plain program's by a relative error of at most 0.0053.
Values may be sent and summed in bfloat16 or wider, within the bound.
A program may use at most 128 MiB of HBM per device.

v0:
```python
import functools

import jax
import jax.numpy as jnp
from jax import lax
from jax.experimental import pallas as pl
from jax.experimental.pallas import tpu as pltpu
from jax.sharding import PartitionSpec as P

MESH = pl.DeviceIdType.MESH
LANES = 128


def ceil_to(value, unit):
    return -(-value // unit) * unit


def phi(diff):
    return diff * lax.rsqrt(diff * diff + jnp.float32(0.25))


def kernel(
    dims,
    table,
    weight,
    x_ref,
    obs_ref,
    w1_ref,
    b1_ref,
    w2_ref,
    b2_ref,
    o_ref,
    taps_ref,
    acc,
    halo1,
    hid,
    halo2,
    pred,
    gath,
    grad,
    hs_sem,
    hr_sem,
    ps_sem,
    pr_sem,
    gs_sem,
    gr_sem,
):
    n_s, n_e, mem, rows, cp, lon, lp, taps, lt = dims
    reach = (taps - 1) // 2
    half = (lt - 1) // 2
    q = rows // n_e
    wide = mem * lp
    sp = lax.axis_index("space")
    en = lax.axis_index("ens")
    has_prev = sp > 0
    has_next = sp < n_s - 1

    def at_prev():
        return {"space": sp - 1, "ens": en}

    def at_next():
        return {"space": sp + 1, "ens": en}

    def peer(k):
        return lax.rem(en + k, n_e)

    barrier = pltpu.get_barrier_semaphore()

    @pl.when(has_prev)
    def _():
        pl.semaphore_signal(barrier, inc=1, device_id=at_prev(), device_id_type=MESH)

    @pl.when(has_next)
    def _():
        pl.semaphore_signal(barrier, inc=1, device_id=at_next(), device_id_type=MESH)

    for k in range(1, n_e):
        pl.semaphore_signal(
            barrier, inc=1, device_id={"space": sp, "ens": peer(k)}, device_id_type=MESH
        )
    count = n_e - 1 + jnp.where(has_prev, 1, 0) + jnp.where(has_next, 1, 0)
    pl.semaphore_wait(barrier, count)

    def halo_up(src, dst, stage):
        return pltpu.make_async_remote_copy(
            src_ref=src.at[pl.ds(0, reach)],
            dst_ref=dst.at[1],
            send_sem=hs_sem.at[stage, 0],
            recv_sem=hr_sem.at[stage, 0],
            device_id=at_prev(),
            device_id_type=MESH,
        )

    def halo_down(src, dst, stage):
        return pltpu.make_async_remote_copy(
            src_ref=src.at[pl.ds(rows - reach, reach)],
            dst_ref=dst.at[0],
            send_sem=hs_sem.at[stage, 1],
            recv_sem=hr_sem.at[stage, 1],
            device_id=at_next(),
            device_id_type=MESH,
        )

    def send_halo(src, dst, stage):
        @pl.when(has_prev)
        def _():
            halo_up(src, dst, stage).start()

        @pl.when(has_next)
        def _():
            halo_down(src, dst, stage).start()

    def recv_halo(src, dst, stage):
        @pl.when(has_prev)
        def _():
            halo_down(src, dst, stage).wait_recv()

        @pl.when(has_next)
        def _():
            halo_up(src, dst, stage).wait_recv()

        @pl.when(jnp.logical_not(has_prev))
        def _():
            dst[0] = jnp.zeros(dst.shape[1:], dst.dtype)

        @pl.when(jnp.logical_not(has_next))
        def _():
            dst[1] = jnp.zeros(dst.shape[1:], dst.dtype)

    def sent_halo(src, dst, stage):
        @pl.when(has_prev)
        def _():
            halo_up(src, dst, stage).wait_send()

        @pl.when(has_next)
        def _():
            halo_down(src, dst, stage).wait_send()

    def build(row, value):
        for mm in range(mem):
            part = value[:, mm * lp : (mm + 1) * lp]
            for s in range(lt):
                d = s - half
                moved = part if d == 0 else pltpu.roll(part, (-d) % lp, 1)
                taps_ref[row, pl.ds(s * cp, cp), pl.ds(mm * lp, lp)] = moved.astype(jnp.bfloat16)

    def conv_rows(w_ref, order):
        step = 256

        def body(n, carry):
            lane = pl.ds(pl.multiple_of(n * step, step), step)
            for r in order:
                lo, hi = max(0, r - rows + 1), min(taps - 1, r)
                y = jnp.dot(
                    w_ref[lo * cp : (hi + 1) * cp, :],
                    taps_ref[r, :, lane],
                    preferred_element_type=jnp.float32,
                )
                for t in range(lo, hi + 1):
                    i = r - t
                    acc[i, :, lane] += table[t, i] * y[(t - lo) * cp : (t - lo + 1) * cp]
            return carry

        lax.fori_loop(0, wide // step, body, 0)

    def conv(own, halo, w_ref, stage):
        acc[...] = jnp.zeros(acc.shape, jnp.float32)

        def own_row(r, carry):
            build(reach + r, own[r].astype(jnp.float32))
            return carry

        lax.fori_loop(0, rows, own_row, 0)
        conv_rows(w_ref, range(reach, reach + rows))
        recv_halo(own, halo, stage)

        def rim_row(r, carry):
            build(r, halo[0, r].astype(jnp.float32))
            build(reach + rows + r, halo[1, r].astype(jnp.float32))
            return carry

        lax.fori_loop(0, reach, rim_row, 0)
        conv_rows(w_ref, list(range(reach)) + list(range(reach + rows, 2 * reach + rows)))

    send_halo(x_ref, halo1, 0)
    conv(x_ref, halo1, w1_ref, 0)

    last = lp - LANES
    tail = lon - last

    def hidden_row(i, carry):
        for mm in range(mem):
            base = mm * lp
            h = jax.nn.gelu(acc[i, :, pl.ds(base, lp)] + b1_ref[...])
            first, end = h[:, :LANES], h[:, last:]
            spot = lax.broadcasted_iota(jnp.int32, end.shape, 1)
            after = pltpu.roll(first, tail, 1)
            before = pltpu.roll(end, LANES - tail, 1)
            wrap = jnp.where(spot < tail, end, jnp.where(spot < tail + half, after, before))
            hid[i, :, pl.ds(base, last)] = h[:, :last].astype(jnp.bfloat16)
            hid[i, :, pl.ds(base + last, LANES)] = wrap.astype(jnp.bfloat16)
        return carry

    lax.fori_loop(0, rows, hidden_row, 0)
    send_halo(hid, halo2, 1)
    conv(hid, halo2, w2_ref, 1)

    def pred_row(i, carry):
        for mm in range(mem):
            lane = pl.ds(mm * lp, lp)
            total = x_ref[i, :, lane].astype(jnp.float32) + acc[i, :, lane] + b2_ref[...]
            pred[i, :, lane] = total.astype(jnp.bfloat16)
        return carry

    lax.fori_loop(0, rows, pred_row, 0)

    def pred_copy(k, j, src_dev, dst_dev):
        return pltpu.make_async_remote_copy(
            src_ref=pred.at[dst_dev * q + j],
            dst_ref=gath.at[src_dev, j],
            send_sem=ps_sem.at[k, j],
            recv_sem=pr_sem.at[k, j],
            device_id={"space": sp, "ens": dst_dev},
            device_id_type=MESH,
        )

    def grad_copy(k, j, src_dev, dst_dev):
        return pltpu.make_async_remote_copy(
            src_ref=grad.at[dst_dev, j],
            dst_ref=o_ref.at[src_dev * q + j],
            send_sem=gs_sem.at[k, j],
            recv_sem=gr_sem.at[k, j],
            device_id={"space": sp, "ens": dst_dev},
            device_id_type=MESH,
        )

    for j in range(q):
        for k in range(1, n_e):
            pred_copy(k, j, en, peer(k)).start()
    for j in range(q):
        gath[en, j] = pred[en * q + j]
    members = n_e * mem
    for j in range(q):
        for k in range(1, n_e):
            pred_copy(k, j, peer(n_e - k), peer(k)).wait_recv()
        scale = weight[0, en * q + j]

        def part(step, carry):
            group, tile = step // (lp // LANES), step % (lp // LANES)
            chan = pl.ds(pl.multiple_of(group * 16, 16), 16)
            spots = [
                (a // mem, pl.ds(pl.multiple_of((a % mem) * lp + tile * LANES, LANES), LANES))
                for a in range(members)
            ]
            vals = [gath[dev, j, chan, lane].astype(jnp.float32) for dev, lane in spots]
            goal = obs_ref[
                j, chan, pl.ds(pl.multiple_of(tile * LANES, LANES), LANES)
            ].astype(jnp.float32)
            sums = [jnp.zeros((16, LANES), jnp.float32) for _ in range(members)]
            for a in range(members):
                for b in range(a + 1, members):
                    d = phi(vals[a] - vals[b])
                    sums[a] = sums[a] + d
                    sums[b] = sums[b] - d
            for a, (dev, lane) in enumerate(spots):
                g = phi(vals[a] - goal) - sums[a] * jnp.float32(1.0 / (members - 1))
                grad[dev, j, chan, lane] = (g * scale).astype(jnp.bfloat16)
            return carry

        lax.fori_loop(0, (cp // 16) * (lp // LANES), part, 0)
        for k in range(1, n_e):
            grad_copy(k, j, en, peer(k)).start()
        o_ref[en * q + j] = grad[en, j]
    sent_halo(x_ref, halo1, 0)
    sent_halo(hid, halo2, 1)
    for j in range(q):
        for k in range(1, n_e):
            pred_copy(k, j, en, peer(k)).wait_send()
            grad_copy(k, j, peer(n_e - k), peer(k)).wait_recv()
            grad_copy(k, j, en, peer(k)).wait_send()


def band_table(band_offset, band_width, taps):
    reach = (taps - 1) // 2
    rel = lax.broadcasted_iota(jnp.int32, (taps, band_offset.shape[0]), 0) - reach
    inside = (rel >= band_offset[None, :]) & (rel < band_offset[None, :] + band_width[None, :])
    scale = lax.rsqrt(band_width.astype(jnp.float32))[None, :]
    return jnp.where(inside, scale, jnp.float32(0.0))


def local(fields, observed, kernel_one, bias_one, kernel_two, bias_two, band_offset, band_width):
    mem, chan, rows, lon = fields.shape
    taps, _, lt, _ = kernel_one.shape
    reach, half = (taps - 1) // 2, (lt - 1) // 2
    n_s, n_e = lax.axis_size("space"), lax.axis_size("ens")
    q = rows // n_e
    cp, lp = ceil_to(chan, 16), ceil_to(lon + 2 * half, LANES)
    sp, en = lax.axis_index("space"), lax.axis_index("ens")
    base = sp * rows

    offset = lax.dynamic_slice_in_dim(band_offset, base, rows, 0)
    width = lax.dynamic_slice_in_dim(band_width, base, rows, 0)
    table = band_table(offset, width, taps)
    glob_rows = (base + lax.iota(jnp.int32, rows)).astype(jnp.float32)
    weight = jnp.cos(jnp.pi * (glob_rows + 0.5) / (rows * n_s) - jnp.pi / 2)[None]

    x = jnp.transpose(fields, (2, 1, 0, 3))
    gap = jnp.zeros((rows, chan, mem, lp - lon - 2 * half), x.dtype)
    x = jnp.concatenate([x, x[..., :half], gap, x[..., lon - half :]], axis=3)
    x = jnp.pad(x, ((0, 0), (0, cp - chan), (0, 0), (0, 0))).reshape(rows, cp, mem * lp)
    obs = lax.dynamic_slice_in_dim(observed, en * q, q, 1)
    obs = jnp.pad(jnp.transpose(obs, (1, 0, 2)), ((0, 0), (0, cp - chan), (0, lp - lon)))

    def flat(w):
        w = jnp.pad(w, ((0, 0), (0, cp - chan), (0, 0), (0, cp - chan)))
        return w.reshape(taps * cp, lt * cp)

    def column(b):
        return jnp.pad(b, (0, cp - chan))[:, None]

    dims = (n_s, n_e, mem, rows, cp, lon, lp, taps, lt)
    wide = mem * lp
    vmem = pl.BlockSpec(memory_space=pltpu.VMEM)
    smem = pl.BlockSpec(memory_space=pltpu.SMEM)
    bf16 = jnp.bfloat16
    out = pl.pallas_call(
        functools.partial(kernel, dims),
        out_shape=jax.ShapeDtypeStruct((rows, cp, wide), bf16),
        in_specs=[smem, smem] + [vmem] * 6,
        out_specs=vmem,
        scratch_shapes=[
            pltpu.VMEM((rows + 2 * reach, lt * cp, wide), bf16),
            pltpu.VMEM((rows, cp, wide), jnp.float32),
            pltpu.VMEM((2, reach, cp, wide), bf16),
            pltpu.VMEM((rows, cp, wide), bf16),
            pltpu.VMEM((2, reach, cp, wide), bf16),
            pltpu.VMEM((rows, cp, wide), bf16),
            pltpu.VMEM((n_e, q, cp, wide), bf16),
            pltpu.VMEM((n_e, q, cp, wide), bf16),
            pltpu.SemaphoreType.DMA((2, 2)),
            pltpu.SemaphoreType.DMA((2, 2)),
            pltpu.SemaphoreType.DMA((n_e, q)),
            pltpu.SemaphoreType.DMA((n_e, q)),
            pltpu.SemaphoreType.DMA((n_e, q)),
            pltpu.SemaphoreType.DMA((n_e, q)),
        ],
        compiler_params=pltpu.CompilerParams(
            collective_id=0, has_side_effects=True, vmem_limit_bytes=40 * 1024 * 1024
        ),
    )(
        table,
        weight,
        x,
        obs,
        flat(kernel_one),
        column(bias_one),
        flat(kernel_two),
        column(bias_two),
    )
    out = out.reshape(rows, cp, mem, lp)[:, :chan, :, :lon]
    return jnp.transpose(out, (2, 1, 0, 3))


def solution(mesh):
    in_specs = (P("ens", None, "space", None), P(None, "space", None), P(), P(), P(), P(), P(), P())
    out_specs = P("ens", None, "space", None)
    return jax.shard_map(local, mesh=mesh, in_specs=in_specs, out_specs=out_specs, check_vma=False)
```

profile of v0, /device:TPU:11, one launch (start us, length us, event | category | flops | bytes accessed | tf_op | source)
XLA Modules:
  0.0 59.1 jit_solution(14834988665811001771)
XLA Ops:
  0.0 0.0 copy-start
  0.0 0.0 copy-start.1
  0.0 0.8 %dynamic-slice_add_fusion = (s32[8]{0:T(128)S(1)}, s32[8]{0:T(128)S(1)}) fusion(s32[64]{0:T(128)} %param.15, s32[]{:T(128)S(6)} %select_n.11, s32[64]{0:T(128)} %param.14), kind=kLoop, calls=%fused_computation.10 | loop fusion | flops 8 | bytes 132 | tf_op jit(solution)/shard_map/add | solution.py:286
  0.8 0.7 %convert_rsqrt_fusion = f32[8]{0:T(128)S(1)} fusion(s32[64]{0:T(128)} %param.15, s32[]{:T(128)S(6)} %select_n.11), kind=kLoop, calls=%fused_computation.7 | loop fusion | flops 8 | bytes 68 | tf_op jit(solution)/shard_map/rsqrt | solution.py:287
  1.6 0.1 and_select_fusion.table
  1.6 0.0 copy-done
  1.6 0.1 constant_dynamic-slice_fusion
  1.8 1.1 %fusion = (bf16[8,45,2,2]{3,0,1,2:T(8,128)(2,1)S(1)}, bf16[8,45,2,2]{3,0,1,2:T(8,128)(2,1)S(1)}) fusion(bf16[8,45,2,360]{3,0,1,2:T(8,128)(2,1)} %bitcast.11), kind=kLoop, calls=%fused_computation.11 | loop fusion | bytes 11520 | tf_op jit(solution)/shard_map/slice | solution.py:309
  2.9 0.1 pad.30.clone
  3.0 0.0 copy-done.1
  3.0 0.3 pad_maximum_fusion
  3.3 0.4 copy.25
  3.7 0.0 copy-start.2
  3.7 0.4 pad.22.clone
  4.1 0.4 reshape.38.x_ref
  4.6 0.2 copy-done.2
  4.7 0.2 copy.26
  5.0 0.2 pad.24.clone
  5.2 0.0 copy-start.3
  5.2 0.4 reshape.39.w1_ref
  5.7 0.6 %copy-done.3 = bf16[9,45,5,45]{3,1,2,0:T(8,128)(2,1)S(1)} copy-done((bf16[9,45,5,45]{3,1,2,0:T(8,128)(2,1)S(1)}, bf16[9,45,5,45]{3,1,2,0:T(8,128)(2,1)}, u32[]{:S(2)}) %copy-start.3) | copy-done | bytes 182274
  6.3 0.2 copy.27
  6.5 0.2 pad.26.clone
  6.7 0.0 copy-start.4
  6.7 0.0 copy-start.5
  6.7 0.4 reshape.40.w2_ref
  7.2 0.2 copy-done.4
  7.4 0.1 copy.20.b1_ref
  7.5 0.0 copy-done.5
  7.5 0.1 copy.21.b2_ref
  7.6 50.1 %shard_map.82 = bf16[8,48,768]{2,1,0:T(8,128)(2,1)S(1)} custom-call(f32[9,8]{1,0:T(8,128)S(1)} %and_select_fusion.table, f32[1,8]{1,0:T(1,128)S(1)} %add_cosine_fusion.weight, bf16[8,48,768]{2,1,0:T(8,128)(2,1)S(1)} %reshape.38.x_ref, bf16[2,48,384]{2,1,0:T(8,128)(2,1)S(1)} %pad.23.obs_ref, bf16[432,240]{1,0:T(8,128)(2,1)S(1)} %reshape.39.w1_ref, ...), custom_call_target="tpu_custom_call" | custom-call | tf_op jit(solution)/shard_map/pallas_call | solution.py:326
  57.7 0.1 reshape.41
  57.8 0.4 slice.14
  58.2 0.9 %copy.30 = bf16[8,45,2,360]{3,0,1,2:T(8,128)(2,1)} copy(bf16[8,45,2,360]{3,2,1,0:T(2,128)(2,1)S(1)} %slice.14) | data formatting | bytes 1036800
  (7 shorter events, 0.1 us)
Async XLA Ops:
  0.0 1.6 %copy-start = (bf16[45,8,360]{2,1,0:T(8,128)(2,1)S(1)}, bf16[45,8,360]{2,1,0:T(8,128)(2,1)}, u32[]{:S(2)}) copy-start(bf16[45,8,360]{2,1,0:T(8,128)(2,1)} %param.9) | copy-start | bytes 777604
  0.0 3.0 %copy-start.1 = (bf16[2,45,8,360]{3,2,1,0:T(8,128)(2,1)S(1)}, bf16[2,45,8,360]{3,2,1,0:T(8,128)(2,1)}, u32[]{:S(2)}) copy-start(bf16[2,45,8,360]{3,2,1,0:T(8,128)(2,1)} %param.8) | copy-start | bytes 1555204
  3.7 1.1 %copy-start.2 = (bf16[9,45,5,45]{3,1,2,0:T(8,128)(2,1)S(1)}, bf16[9,45,5,45]{3,1,2,0:T(8,128)(2,1)}, u32[]{:S(2)}) copy-start(bf16[9,45,5,45]{3,1,2,0:T(8,128)(2,1)} %param.10) | copy-start | bytes 546754
  5.2 1.1 %copy-start.3 = (bf16[9,45,5,45]{3,1,2,0:T(8,128)(2,1)S(1)}, bf16[9,45,5,45]{3,1,2,0:T(8,128)(2,1)}, u32[]{:S(2)}) copy-start(bf16[9,45,5,45]{3,1,2,0:T(8,128)(2,1)} %param.12) | copy-start | bytes 546754
  6.7 0.7 %copy-start.4 = (f32[45]{0:T(128)S(1)}, f32[45]{0:T(128)}, u32[]{:S(2)}) copy-start(f32[45]{0:T(128)} %param.11) | copy-start | bytes 544
  6.7 0.7 %copy-start.5 = (f32[45]{0:T(128)S(1)}, f32[45]{0:T(128)}, u32[]{:S(2)}) copy-start(f32[45]{0:T(128)} %param.13) | copy-start | bytes 544
where the time goes:
time: 59.3 us; the launch traced here: 59.1 us
  Pallas kernels  50.1 us (84%)
  local copies, waits for them, and re-layouts  6.89 us (12%)
  other arithmetic  1.93 us (3%)
    pallas_call x1, Pallas kernels, local(): pl.pallas_call(functools.partial(kernel, dims), out_shape=jax.ShapeDtypeS...  50.1 us
    unnamed x17, local copies, waits for them, and re-layouts  2.73 us

commit v1 on v0

v1 whole, which is shorter than its diff:
```python
import functools

import jax
import jax.numpy as jnp
from jax import lax
from jax.experimental import pallas as pl
from jax.experimental.pallas import tpu as pltpu
from jax.sharding import PartitionSpec as P

MESH = pl.DeviceIdType.MESH
LANES = 128


def ceil_to(value, unit):
    return -(-value // unit) * unit


def phi(diff):
    return diff * lax.rsqrt(diff * diff + jnp.float32(0.25))


def kernel(
    dims,
    offset,
    width,
    weight,
    x_ref,
    obs_ref,
    w1_ref,
    b1_ref,
    w2_ref,
    b2_ref,
    o_ref,
    flat1,
    flat2,
    taps_ref,
    acc,
    halo1,
    hid,
    halo2,
    pred,
    gath,
    grad,
    hs_sem,
    hr_sem,
    ps_sem,
    pr_sem,
    gs_sem,
    gr_sem,
):
    n_s, n_e, mem, rows, cp, lon, lp, taps, lt = dims
    reach = (taps - 1) // 2
    half = (lt - 1) // 2
    q = rows // n_e
    sp = lax.axis_index("space")
    en = lax.axis_index("ens")
    has_prev = sp > 0
    has_next = sp < n_s - 1

    def at_prev():
        return {"space": sp - 1, "ens": en}

    def at_next():
        return {"space": sp + 1, "ens": en}

    def peer(k):
        return lax.rem(en + k, n_e)

    barrier = pltpu.get_barrier_semaphore()

    @pl.when(has_prev)
    def _():
        pl.semaphore_signal(barrier, inc=1, device_id=at_prev(), device_id_type=MESH)

    @pl.when(has_next)
    def _():
        pl.semaphore_signal(barrier, inc=1, device_id=at_next(), device_id_type=MESH)

    for k in range(1, n_e):
        pl.semaphore_signal(
            barrier, inc=1, device_id={"space": sp, "ens": peer(k)}, device_id_type=MESH
        )
    count = n_e - 1 + jnp.where(has_prev, 1, 0) + jnp.where(has_next, 1, 0)
    pl.semaphore_wait(barrier, count)

    def halo_up(src, dst, stage, mm):
        return pltpu.make_async_remote_copy(
            src_ref=src.at[mm, pl.ds(0, reach)],
            dst_ref=dst.at[mm, 1],
            send_sem=hs_sem.at[stage, 0, mm],
            recv_sem=hr_sem.at[stage, 0, mm],
            device_id=at_prev(),
            device_id_type=MESH,
        )

    def halo_down(src, dst, stage, mm):
        return pltpu.make_async_remote_copy(
            src_ref=src.at[mm, pl.ds(rows - reach, reach)],
            dst_ref=dst.at[mm, 0],
            send_sem=hs_sem.at[stage, 1, mm],
            recv_sem=hr_sem.at[stage, 1, mm],
            device_id=at_next(),
            device_id_type=MESH,
        )

    def send_halo(src, dst, stage, mm):
        @pl.when(has_prev)
        def _():
            halo_up(src, dst, stage, mm).start()

        @pl.when(has_next)
        def _():
            halo_down(src, dst, stage, mm).start()

    def recv_halo(src, dst, stage, mm):
        @pl.when(has_prev)
        def _():
            halo_down(src, dst, stage, mm).wait_recv()

        @pl.when(has_next)
        def _():
            halo_up(src, dst, stage, mm).wait_recv()

        @pl.when(jnp.logical_not(has_prev))
        def _():
            dst[mm, 0] = jnp.zeros(dst.shape[2:], dst.dtype)

        @pl.when(jnp.logical_not(has_next))
        def _():
            dst[mm, 1] = jnp.zeros(dst.shape[2:], dst.dtype)

    def sent_halo(src, dst, stage, mm):
        @pl.when(has_prev)
        def _():
            halo_up(src, dst, stage, mm).wait_send()

        @pl.when(has_next)
        def _():
            halo_down(src, dst, stage, mm).wait_send()

    last = lp - LANES
    tail = lon - last

    def build(mm, row, value):
        first, end = value[:, :LANES], value[:, last:]
        spot = lax.broadcasted_iota(jnp.int32, end.shape, 1)
        after = pltpu.roll(first, tail, 1)
        before = pltpu.roll(end, LANES - tail, 1)
        wrap = jnp.where(spot < tail, end, jnp.where(spot < tail + half, after, before))
        whole = jnp.concatenate([value[:, :last], wrap], axis=1)
        for s in range(lt):
            d = s - half
            moved = whole if d == 0 else pltpu.roll(whole, (-d) % lp, 1)
            taps_ref[mm, row, pl.ds(s * cp, cp), :] = moved.astype(jnp.bfloat16)

    def flatten(w_ref, flat):
        deep = flat.shape[1]

        def one(t, carry):
            rowblock = jnp.zeros((cp, deep), jnp.float32)
            for s in range(lt):
                block = w_ref[t, s].astype(jnp.float32)
                block = jnp.concatenate(
                    [block, jnp.zeros((cp, deep - block.shape[1]), jnp.float32)], axis=1
                )
                rowblock += pltpu.roll(block, s * cp, 1) if s else block
            flat[pl.ds(pl.multiple_of(t * cp, cp), cp), :] = rowblock.astype(jnp.bfloat16)
            return carry

        lax.fori_loop(0, taps, one, 0)

    def inside(t, i):
        first = offset[sp * rows + i]
        return jnp.where(
            jnp.logical_and(t - reach >= first, t - reach < first + width[sp * rows + i]), 1.0, 0.0
        ).astype(jnp.float32)

    def conv_rows(flat, mm, order):
        for r in order:
            lo, hi = max(0, r - rows + 1), min(taps - 1, r)
            y = jnp.dot(
                flat[lo * cp : (hi + 1) * cp, : lt * cp],
                taps_ref[mm, r],
                preferred_element_type=jnp.float32,
            )
            for t in range(lo, hi + 1):
                i = r - t
                acc[mm, i] += inside(t, i) * y[(t - lo) * cp : (t - lo + 1) * cp]

    def conv_own(own, flat, mm):
        acc[mm] = jnp.zeros(acc.shape[1:], jnp.float32)

        def own_row(r, carry):
            build(mm, reach + r, own[mm, r].astype(jnp.float32))
            return carry

        lax.fori_loop(0, rows, own_row, 0)
        conv_rows(flat, mm, range(reach, reach + rows))

    def conv_rim(halo, flat, mm):
        def rim_row(r, carry):
            build(mm, r, halo[mm, 0, r].astype(jnp.float32))
            build(mm, reach + rows + r, halo[mm, 1, r].astype(jnp.float32))
            return carry

        lax.fori_loop(0, reach, rim_row, 0)
        conv_rows(flat, mm, list(range(reach)) + list(range(reach + rows, 2 * reach + rows)))

    def scaled(mm, i):
        wide = jnp.full((8, LANES), width[sp * rows + i], jnp.int32).astype(jnp.float32)
        return acc[mm, i] * lax.rsqrt(wide)[:1, :1]

    def each(count, body):
        def step(index, carry):
            body(index)
            return carry

        lax.fori_loop(0, count, step, 0)

    def pred_copy(k, j, mm, src_dev, dst_dev):
        return pltpu.make_async_remote_copy(
            src_ref=pred.at[mm, dst_dev * q + j],
            dst_ref=gath.at[src_dev, mm, j],
            send_sem=ps_sem.at[k, j, mm],
            recv_sem=pr_sem.at[k, j, mm],
            device_id={"space": sp, "ens": dst_dev},
            device_id_type=MESH,
        )

    def grad_copy(k, j, mm, src_dev, dst_dev):
        return pltpu.make_async_remote_copy(
            src_ref=grad.at[dst_dev, mm, j],
            dst_ref=o_ref.at[mm, src_dev * q + j],
            send_sem=gs_sem.at[k, j, mm],
            recv_sem=gr_sem.at[k, j, mm],
            device_id={"space": sp, "ens": dst_dev},
            device_id_type=MESH,
        )

    for mm in range(mem):
        send_halo(x_ref, halo1, 0, mm)
    flatten(w1_ref, flat1)
    each(mem, lambda mm: conv_own(x_ref, flat1, mm))
    flatten(w2_ref, flat2)
    for mm in range(mem):
        recv_halo(x_ref, halo1, 0, mm)
        conv_rim(halo1, flat1, mm)

        def hidden_row(i):
            hid[mm, i] = jax.nn.gelu(scaled(mm, i) + b1_ref[...]).astype(jnp.bfloat16)

        each(rows, hidden_row)
        send_halo(hid, halo2, 1, mm)
    each(mem, lambda mm: conv_own(hid, flat2, mm))
    for mm in range(mem):
        recv_halo(hid, halo2, 1, mm)
        conv_rim(halo2, flat2, mm)

        def pred_row(i):
            total = x_ref[mm, i].astype(jnp.float32) + scaled(mm, i) + b2_ref[...]
            pred[mm, i] = total.astype(jnp.bfloat16)

        each(rows, pred_row)
        for j in range(q):
            for k in range(1, n_e):
                pred_copy(k, j, mm, en, peer(k)).start()
        for j in range(q):
            gath[en, mm, j] = pred[mm, en * q + j]
    members = n_e * mem
    for j in range(q):
        for k in range(1, n_e):
            for mm in range(mem):
                pred_copy(k, j, mm, peer(n_e - k), peer(k)).wait_recv()
        scale = weight[0, en * q + j]

        def part(step, carry):
            group, tile = step // (lp // LANES), step % (lp // LANES)
            chan = pl.ds(pl.multiple_of(group * 16, 16), 16)
            lane = pl.ds(pl.multiple_of(tile * LANES, LANES), LANES)
            spots = [(a // mem, a % mem) for a in range(members)]
            vals = [gath[dev, mm, j, chan, lane].astype(jnp.float32) for dev, mm in spots]
            goal = obs_ref[j, chan, lane].astype(jnp.float32)
            sums = [jnp.zeros((16, LANES), jnp.float32) for _ in range(members)]
            for a in range(members):
                for b in range(a + 1, members):
                    d = phi(vals[a] - vals[b])
                    sums[a] = sums[a] + d
                    sums[b] = sums[b] - d
            for a, (dev, mm) in enumerate(spots):
                g = phi(vals[a] - goal) - sums[a] * jnp.float32(1.0 / (members - 1))
                grad[dev, mm, j, chan, lane] = (g * scale).astype(jnp.bfloat16)
            return carry

        lax.fori_loop(0, (cp // 16) * (lp // LANES), part, 0)
        for k in range(1, n_e):
            for mm in range(mem):
                grad_copy(k, j, mm, en, peer(k)).start()
        for mm in range(mem):
            o_ref[mm, en * q + j] = grad[en, mm, j]
    for mm in range(mem):
        sent_halo(x_ref, halo1, 0, mm)
        sent_halo(hid, halo2, 1, mm)
        for j in range(q):
            for k in range(1, n_e):
                pred_copy(k, j, mm, en, peer(k)).wait_send()
                grad_copy(k, j, mm, peer(n_e - k), peer(k)).wait_recv()
                grad_copy(k, j, mm, en, peer(k)).wait_send()


def local(fields, observed, kernel_one, bias_one, kernel_two, bias_two, band_offset, band_width):
    mem, chan, rows, lon = fields.shape
    taps, _, lt, _ = kernel_one.shape
    reach, half = (taps - 1) // 2, (lt - 1) // 2
    n_s, n_e = lax.axis_size("space"), lax.axis_size("ens")
    q = rows // n_e
    cp, lp = ceil_to(chan, 16), ceil_to(lon + 2 * half, LANES)
    sp, en = lax.axis_index("space"), lax.axis_index("ens")
    base = sp * rows

    glob_rows = (base + lax.iota(jnp.int32, rows)).astype(jnp.float32)
    weight = jnp.cos(jnp.pi * (glob_rows + 0.5) / (rows * n_s) - jnp.pi / 2)[None]

    x = jnp.transpose(fields, (0, 2, 1, 3))
    x = jnp.pad(x, ((0, 0), (0, 0), (0, cp - chan), (0, lp - lon)))
    obs = lax.dynamic_slice_in_dim(observed, en * q, q, 1)
    obs = jnp.pad(jnp.transpose(obs, (1, 0, 2)), ((0, 0), (0, cp - chan), (0, lp - lon)))

    def blocks(w):
        w = jnp.transpose(w, (0, 2, 1, 3))
        return jnp.pad(w, ((0, 0), (0, 0), (0, cp - chan), (0, LANES - chan)))

    def column(b):
        return jnp.pad(b, (0, cp - chan))[:, None]

    dims = (n_s, n_e, mem, rows, cp, lon, lp, taps, lt)
    vmem = pl.BlockSpec(memory_space=pltpu.VMEM)
    smem = pl.BlockSpec(memory_space=pltpu.SMEM)
    bf16 = jnp.bfloat16
    deep = ceil_to(lt * cp, LANES)
    out = pl.pallas_call(
        functools.partial(kernel, dims),
        out_shape=jax.ShapeDtypeStruct((mem, rows, cp, lp), bf16),
        in_specs=[smem] * 3 + [vmem] * 6,
        out_specs=vmem,
        scratch_shapes=[
            pltpu.VMEM((taps * cp, deep), bf16),
            pltpu.VMEM((taps * cp, deep), bf16),
            pltpu.VMEM((mem, rows + 2 * reach, lt * cp, lp), bf16),
            pltpu.VMEM((mem, rows, cp, lp), jnp.float32),
            pltpu.VMEM((mem, 2, reach, cp, lp), bf16),
            pltpu.VMEM((mem, rows, cp, lp), bf16),
            pltpu.VMEM((mem, 2, reach, cp, lp), bf16),
            pltpu.VMEM((mem, rows, cp, lp), bf16),
            pltpu.VMEM((n_e, mem, q, cp, lp), bf16),
            pltpu.VMEM((n_e, mem, q, cp, lp), bf16),
            pltpu.SemaphoreType.DMA((2, 2, mem)),
            pltpu.SemaphoreType.DMA((2, 2, mem)),
            pltpu.SemaphoreType.DMA((n_e, q, mem)),
            pltpu.SemaphoreType.DMA((n_e, q, mem)),
            pltpu.SemaphoreType.DMA((n_e, q, mem)),
            pltpu.SemaphoreType.DMA((n_e, q, mem)),
        ],
        compiler_params=pltpu.CompilerParams(
            collective_id=0, has_side_effects=True, vmem_limit_bytes=40 * 1024 * 1024
        ),
    )(
        band_offset,
        band_width,
        weight,
        x,
        obs,
        blocks(kernel_one),
        column(bias_one),
        blocks(kernel_two),
        column(bias_two),
    )
    return jnp.transpose(out[:, :, :chan, :lon], (0, 2, 1, 3))


def solution(mesh):
    in_specs = (P("ens", None, "space", None), P(None, "space", None), P(), P(), P(), P(), P(), P())
    out_specs = P("ens", None, "space", None)
    return jax.shard_map(local, mesh=mesh, in_specs=in_specs, out_specs=out_specs, check_vma=False)
```

time: 59.3 us -> 55.1 us (0.929)
  the two profiles are of different devices: /device:TPU:11 before, /device:TPU:0 now
where the time goes in v1:
time: 55.1 us; the launch traced here: 54.9 us
  Pallas kernels  49.1 us (89%)
  local copies, waits for them, and re-layouts  5.61 us (10%)
    pallas_call x1, Pallas kernels, local(): pl.pallas_call(functools.partial(kernel, dims), out_shape=jax.ShapeDtypeS...  49.1 us
    unnamed x16, local copies, waits for them, and re-layouts  2.93 us
    pad x2, local copies, waits for them, and re-layouts, blocks(): return jnp.pad(w, ((0, 0), (0, 0), (0, cp - chan), (0, LANES - chan)))  1.35 us

profile of v1, /device:TPU:0, one launch (start us, length us, event | category | flops | bytes accessed | tf_op | source)
XLA Modules:
  0.0 54.9 jit_solution(13295625173803974756)
XLA Ops:
  0.0 0.0 copy-start
  0.1 0.0 copy-start.5
  0.1 0.7 %copy-done.5 = f32[45]{0:T(128)S(1)} copy-done((f32[45]{0:T(128)S(1)}, f32[45]{0:T(128)}, u32[]{:S(2)}) %copy-start.5) | copy-done | bytes 204
  0.7 0.0 copy-start.6
  0.8 0.6 %copy-done.6 = f32[45]{0:T(128)S(1)} copy-done((f32[45]{0:T(128)S(1)}, f32[45]{0:T(128)}, u32[]{:S(2)}) %copy-start.6) | copy-done | bytes 204
  1.4 0.1 copy.12.b2_ref
  1.5 0.1 copy.11.b1_ref
  1.6 0.0 copy-done
  1.6 0.1 constant_dynamic-slice_fusion
  1.7 0.0 copy-start.4
  1.7 1.2 %pad.24.w1_ref = bf16[9,5,48,128]{3,2,1,0:T(8,128)(2,1)S(1)} pad(bf16[9,5,45,45]{3,2,1,0:T(8,128)(2,1)} %bitcast.15, bf16[]{:T(256)} %constant.24.clone.1), padding=0_0x0_0x0_3x0_83 | pad | bytes 735212 | tf_op jit(solution)/shard_map/jit(_pad)/pad | solution.py:330
  3.0 0.0 copy-done.4
  3.0 0.0 copy-start.3
  3.0 0.1 pad.26.w2_ref
  3.1 0.9 %copy-done.3 = bf16[2,45,8,360]{3,2,1,0:T(8,128)(2,1)S(1)} copy-done((bf16[2,45,8,360]{3,2,1,0:T(8,128)(2,1)S(1)}, bf16[2,45,8,360]{3,2,1,0:T(8,128)(2,1)}, u32[]{:S(2)}) %copy-start.3) | copy-done | bytes 518424
  4.0 0.1 copy.17
  4.1 0.0 copy-start.1
  4.1 0.0 copy-start.2
  4.1 0.1 pad.22.x_ref
  4.2 0.6 %copy-done.1 = s32[64]{0:T(128)S(1)} copy-done((s32[64]{0:T(128)S(1)}, s32[64]{0:T(128)}, u32[]{:S(2)}) %copy-start.1) | copy-done | bytes 280
  4.8 0.0 copy-done.2
  4.8 49.1 %shard_map.82 = bf16[2,8,48,384]{3,2,1,0:T(8,128)(2,1)S(1)} custom-call(s32[64]{0:T(128)S(1)} %copy-done.1, s32[64]{0:T(128)S(1)} %copy-done.2, f32[1,8]{1,0:T(1,128)S(1)} %add_cosine_fusion.weight, bf16[2,8,48,384]{3,2,1,0:T(8,128)(2,1)S(1)} %pad.22.x_ref, bf16[2,48,384]{2,1,0:T(8,128)(2,1)S(1)} %pad.23.obs_ref, bf16[9,5,48,128]{3,2,1,0:T(8,128)(2,1)S(1)} %pad.24.w1_ref, ...), custom_call_target="tpu_custom_call" | custom-call | tf_op jit(solution)/shard_map/pallas_call | solution.py:340
  53.9 0.1 slice_bitcast_fusion
  54.0 0.9 %copy.13 = bf16[2,45,8,360]{3,2,1,0:T(8,128)(2,1)} copy(bf16[2,45,8,360]{3,1,2,0:T(8,128)(2,1)S(1)} %slice_bitcast_fusion) | data formatting | bytes 1036800 | tf_op jit(solution)/shard_map/transpose | solution.py:377
  (5 shorter events, 0.1 us)
Async XLA Ops:
  0.0 1.6 %copy-start = (bf16[45,8,360]{2,1,0:T(8,128)(2,1)S(1)}, bf16[45,8,360]{2,1,0:T(8,128)(2,1)}, u32[]{:S(2)}) copy-start(bf16[45,8,360]{2,1,0:T(8,128)(2,1)} %param.9) | copy-start | bytes 777604
  0.1 0.7 %copy-start.5 = (f32[45]{0:T(128)S(1)}, f32[45]{0:T(128)}, u32[]{:S(2)}) copy-start(f32[45]{0:T(128)} %param.11) | copy-start | bytes 544
  0.7 0.7 %copy-start.6 = (f32[45]{0:T(128)S(1)}, f32[45]{0:T(128)}, u32[]{:S(2)}) copy-start(f32[45]{0:T(128)} %param.13) | copy-start | bytes 544
  1.7 1.2 %copy-start.4 = (bf16[9,45,5,45]{3,1,2,0:T(8,128)(2,1)S(1)}, bf16[9,45,5,45]{3,1,2,0:T(8,128)(2,1)}, u32[]{:S(2)}) copy-start(bf16[9,45,5,45]{3,1,2,0:T(8,128)(2,1)} %param.12) | copy-start | bytes 546754
  3.0 1.1 %copy-start.3 = (bf16[2,45,8,360]{3,2,1,0:T(8,128)(2,1)S(1)}, bf16[2,45,8,360]{3,2,1,0:T(8,128)(2,1)}, u32[]{:S(2)}) copy-start(bf16[2,45,8,360]{3,2,1,0:T(8,128)(2,1)} %param.8) | copy-start | bytes 1555204
  4.1 0.7 %copy-start.1 = (s32[64]{0:T(128)S(1)}, s32[64]{0:T(128)}, u32[]{:S(2)}) copy-start(s32[64]{0:T(128)} %offset.1) | copy-start | bytes 772
  4.1 0.7 %copy-start.2 = (s32[64]{0:T(128)S(1)}, s32[64]{0:T(128)}, u32[]{:S(2)}) copy-start(s32[64]{0:T(128)} %width.1) | copy-start | bytes 772

commit v2 on v1

--- a/solution.py
+++ b/solution.py
@@ -240,19 +240,19 @@
     for mm in range(mem):
         send_halo(x_ref, halo1, 0, mm)
     flatten(w1_ref, flat1)
-    each(mem, lambda mm: conv_own(x_ref, flat1, mm))
+    for mm in range(mem):
+        conv_own(x_ref, flat1, mm)
+        recv_halo(x_ref, halo1, 0, mm)
+        conv_rim(halo1, flat1, mm)
+
+        def hidden_row(i):
+            hid[mm, i] = jax.nn.gelu(scaled(mm, i) + b1_ref[...]).astype(jnp.bfloat16)
+
+        each(rows, hidden_row)
+        send_halo(hid, halo2, 1, mm)
     flatten(w2_ref, flat2)
     for mm in range(mem):
-        recv_halo(x_ref, halo1, 0, mm)
-        conv_rim(halo1, flat1, mm)
-
-        def hidden_row(i):
-            hid[mm, i] = jax.nn.gelu(scaled(mm, i) + b1_ref[...]).astype(jnp.bfloat16)
-
-        each(rows, hidden_row)
-        send_halo(hid, halo2, 1, mm)
-    each(mem, lambda mm: conv_own(hid, flat2, mm))
-    for mm in range(mem):
+        conv_own(hid, flat2, mm)
         recv_halo(hid, halo2, 1, mm)
         conv_rim(halo2, flat2, mm)
 

time: 55.1 us -> 53 us (0.962)
  the two profiles are of different devices: /device:TPU:0 before, /device:TPU:28 now
where the time goes in v2:
time: 53 us; the launch traced here: 52.8 us
  Pallas kernels  47.1 us (89%)
  local copies, waits for them, and re-layouts  5.61 us (11%)
    pallas_call x1, Pallas kernels, local(): pl.pallas_call(functools.partial(kernel, dims), out_shape=jax.ShapeDtypeS...  47.1 us
    unnamed x16, local copies, waits for them, and re-layouts  2.93 us
    pad x2, local copies, waits for them, and re-layouts, blocks(): return jnp.pad(w, ((0, 0), (0, 0), (0, cp - chan), (0, LANES - chan)))  1.35 us

profile of v2, /device:TPU:28, one launch (start us, length us, event | category | flops | bytes accessed | tf_op | source)
XLA Modules:
  0.0 52.8 jit_solution(10180126004581057191)
XLA Ops:
  0.0 0.0 copy-start
  0.1 0.0 copy-start.5
  0.1 0.7 %copy-done.5 = f32[45]{0:T(128)S(1)} copy-done((f32[45]{0:T(128)S(1)}, f32[45]{0:T(128)}, u32[]{:S(2)}) %copy-start.5) | copy-done | bytes 204
  0.7 0.0 copy-start.6
  0.8 0.6 %copy-done.6 = f32[45]{0:T(128)S(1)} copy-done((f32[45]{0:T(128)S(1)}, f32[45]{0:T(128)}, u32[]{:S(2)}) %copy-start.6) | copy-done | bytes 204
  1.4 0.1 copy.12.b2_ref
  1.5 0.1 copy.11.b1_ref
  1.6 0.0 copy-done
  1.6 0.1 constant_dynamic-slice_fusion
  1.7 0.0 copy-start.4
  1.7 1.2 %pad.24.w1_ref = bf16[9,5,48,128]{3,2,1,0:T(8,128)(2,1)S(1)} pad(bf16[9,5,45,45]{3,2,1,0:T(8,128)(2,1)} %bitcast.15, bf16[]{:T(256)} %constant.24.clone.1), padding=0_0x0_0x0_3x0_83 | pad | bytes 735212 | tf_op jit(solution)/shard_map/jit(_pad)/pad | solution.py:330
  3.0 0.0 copy-done.4
  3.0 0.0 copy-start.3
  3.0 0.1 pad.26.w2_ref
  3.1 0.9 %copy-done.3 = bf16[2,45,8,360]{3,2,1,0:T(8,128)(2,1)S(1)} copy-done((bf16[2,45,8,360]{3,2,1,0:T(8,128)(2,1)S(1)}, bf16[2,45,8,360]{3,2,1,0:T(8,128)(2,1)}, u32[]{:S(2)}) %copy-start.3) | copy-done | bytes 518424
  4.0 0.1 copy.17
  4.1 0.0 copy-start.1
  4.1 0.0 copy-start.2
  4.1 0.1 pad.22.x_ref
  4.2 0.6 %copy-done.1 = s32[64]{0:T(128)S(1)} copy-done((s32[64]{0:T(128)S(1)}, s32[64]{0:T(128)}, u32[]{:S(2)}) %copy-start.1) | copy-done | bytes 280
  4.8 0.0 copy-done.2
  4.8 47.1 %shard_map.82 = bf16[2,8,48,384]{3,2,1,0:T(8,128)(2,1)S(1)} custom-call(s32[64]{0:T(128)S(1)} %copy-done.1, s32[64]{0:T(128)S(1)} %copy-done.2, f32[1,8]{1,0:T(1,128)S(1)} %add_cosine_fusion.weight, bf16[2,8,48,384]{3,2,1,0:T(8,128)(2,1)S(1)} %pad.22.x_ref, bf16[2,48,384]{2,1,0:T(8,128)(2,1)S(1)} %pad.23.obs_ref, bf16[9,5,48,128]{3,2,1,0:T(8,128)(2,1)S(1)} %pad.24.w1_ref, ...), custom_call_target="tpu_custom_call" | custom-call | tf_op jit(solution)/shard_map/pallas_call | solution.py:340
  51.8 0.1 slice_bitcast_fusion
  51.9 0.9 %copy.13 = bf16[2,45,8,360]{3,2,1,0:T(8,128)(2,1)} copy(bf16[2,45,8,360]{3,1,2,0:T(8,128)(2,1)S(1)} %slice_bitcast_fusion) | data formatting | bytes 1036800 | tf_op jit(solution)/shard_map/transpose | solution.py:377
  (5 shorter events, 0.1 us)
Async XLA Ops:
  0.0 1.6 %copy-start = (bf16[45,8,360]{2,1,0:T(8,128)(2,1)S(1)}, bf16[45,8,360]{2,1,0:T(8,128)(2,1)}, u32[]{:S(2)}) copy-start(bf16[45,8,360]{2,1,0:T(8,128)(2,1)} %param.9) | copy-start | bytes 777604
  0.1 0.7 %copy-start.5 = (f32[45]{0:T(128)S(1)}, f32[45]{0:T(128)}, u32[]{:S(2)}) copy-start(f32[45]{0:T(128)} %param.11) | copy-start | bytes 544
  0.7 0.7 %copy-start.6 = (f32[45]{0:T(128)S(1)}, f32[45]{0:T(128)}, u32[]{:S(2)}) copy-start(f32[45]{0:T(128)} %param.13) | copy-start | bytes 544
  1.7 1.2 %copy-start.4 = (bf16[9,45,5,45]{3,1,2,0:T(8,128)(2,1)S(1)}, bf16[9,45,5,45]{3,1,2,0:T(8,128)(2,1)}, u32[]{:S(2)}) copy-start(bf16[9,45,5,45]{3,1,2,0:T(8,128)(2,1)} %param.12) | copy-start | bytes 546754
  3.0 1.1 %copy-start.3 = (bf16[2,45,8,360]{3,2,1,0:T(8,128)(2,1)S(1)}, bf16[2,45,8,360]{3,2,1,0:T(8,128)(2,1)}, u32[]{:S(2)}) copy-start(bf16[2,45,8,360]{3,2,1,0:T(8,128)(2,1)} %param.8) | copy-start | bytes 1555204
  4.1 0.7 %copy-start.1 = (s32[64]{0:T(128)S(1)}, s32[64]{0:T(128)}, u32[]{:S(2)}) copy-start(s32[64]{0:T(128)} %offset.1) | copy-start | bytes 772
  4.1 0.7 %copy-start.2 = (s32[64]{0:T(128)S(1)}, s32[64]{0:T(128)}, u32[]{:S(2)}) copy-start(s32[64]{0:T(128)} %width.1) | copy-start | bytes 772
